TPU v7x, 32 devices: a whole 2x2x4 slice. The times are simulated.
32 devices in a mesh: curve: 8 (over z, x), group: 4 (over y, core).
Axes of the slice: x: 2, y: 2, z: 4, core: 2. Of those that a mesh axis runs over, the one named last changes fastest.
Arguments:
- right_side: float32 [64, 8192], P(None, ('curve', 'group')), may hold values from -6 to 6
- start_field: float32 [64, 8192], P(None, ('curve', 'group')), may hold values from -3 to 3
- block_level: int32 [8192], P(('curve', 'group')), may hold values from 0 to 3
- neighbors: int32 [8, 8192], P(None, ('curve', 'group')), may hold values from -64 to 64, as said below
- neighbor_kinds: int32 [8, 8192], P(None, ('curve', 'group')), may hold values from 0 to 29
- owners_zero: int32 [2, 8192], P(None, ('curve', 'group')), may hold values from 0 to 63, as said below
- owners_one: int32 [2, 2048], P(None, 'curve'), may hold values from 0 to 63, as said below
- owners_two: int32 [2, 512], P(None, 'curve'), may hold values from 0 to 15, as said below
- owners_three: int32 [2, 128], replicated, may hold values from 0 to 7, as said below
- coarse_neighbors: int32 [8, 32], replicated, may hold values from -1 to 31, as said below
- coarse_kinds: int32 [8, 32], replicated, may hold values from 0 to 29
- coarse_level: int32 [32], replicated, may hold values from 0 to 3
- stiffness: float32 [64, 64], replicated
- smoother: float32 [64, 64], replicated
- couplings: float32 [30, 64, 64], replicated, may hold values from -0.18 to 0.18
- restriction: float32 [8, 64, 64], replicated, may hold values from -0.375 to 0.375
Outputs:
- smoothed: float32 [64, 8192], P(None, ('curve', 'group'))
Inputs may be any that keep to these rules, and one draw needn't show every extreme that they name: `neighbors`: 0 where a slot couples to nothing, else the nonzero offset to another fine block inside the grid; in slot 0 the first block of each device's range has offset exactly -64 and the last exactly 64 wherever that neighbour exists. `owners_zero`: row 0: within each device's 256 blocks, slots of 64 level-one blocks that never fall, every slot used by 1 to 8 blocks and by 8 in some; row 1: octant. `owners_one`: row 0: within each curve index's level-one blocks, slots of 64 level-two blocks that never fall, every slot used by 1 to 8 blocks and by 8 in some; row 1: octant. `owners_two`: row 0: within each curve index's 64 blocks, slots of 16 level-three blocks that never fall, every slot used by 1 to 8 blocks and by 8 in some; row 1: octant. `owners_three`: row 0: within each curve index's 16 blocks, slots of 4 level-four blocks that never fall, every slot used by 1 to 8 blocks and by 8 in some; row 1: octant. `coarse_neighbors`: -1 where a slot couples to nothing, else another level-four block.
All inputs are finite; a program needn't handle non-finite values.
Results may differ from a plain program's by a relative error of at most 0.0003.
Values sent between devices are 32-bit elements; how exact they have to be, the bound alone decides.
A program may use at most 64 MiB of HBM per device.

v0:
```python
import functools

import jax
import jax.numpy as jnp
from jax import lax
from jax.experimental import pallas as pl
from jax.experimental.pallas import tpu as pltpu
from jax.sharding import PartitionSpec as P

DAMPING = 0.7
COARSE_SWEEPS = 3
LANES = 128
HALF = 64
F32, BF16 = jnp.float32, jnp.bfloat16
MESH = pl.DeviceIdType.MESH


def split(x):
    hi = x.astype(BF16)
    return hi, (x - hi.astype(F32)).astype(BF16)


def stack(x):
    return jnp.concatenate(split(x), axis=0)


def side(x):
    return jnp.concatenate(split(x), axis=1)


def fold(r):
    n = r.shape[0] // 2
    return (r[:n, :LANES] + r[n:, :LANES]) + r[:n, LANES:]


def times(left, x):
    return fold(jnp.dot(left, side(x), preferred_element_type=F32))


def swap(x):
    return pltpu.roll(x, HALF, 1)


def edge_inner(ref):
    a, b = ref[:, :LANES], ref[:, LANES:]
    low = lax.broadcasted_iota(jnp.int32, a.shape, 1) < HALF
    return jnp.where(low, a, b), swap(jnp.where(low, b, a))


def lane_take(src, lane):
    return jnp.take_along_axis(src, lane, axis=1)


def row_take(ref, row, index):
    got = jnp.zeros(index.shape, jnp.int32)
    width = ref.shape[1]
    for first in range(0, width, LANES):
        size = min(LANES, width - first)
        line = ref[row:row + 1, first:first + size]
        if size < LANES:
            line = jnp.concatenate([line, jnp.zeros((1, LANES - size), jnp.int32)], axis=1)
        tile = jnp.broadcast_to(line, index.shape)
        found = lane_take(tile, index & (LANES - 1))
        got = jnp.where((index >> 7) == first // LANES, found, got)
    return got


def octant_dot(left, x, octant):
    parts = [jnp.where(octant == o, x, 0.0) for o in range(left.shape[1] // x.shape[0])]
    return times(left, jnp.concatenate(parts, axis=0))


def slots_of(parent):
    ids = lax.broadcasted_iota(jnp.int32, (LANES, LANES), 0)
    return jnp.where(ids == parent, 1.0, 0.0).astype(BF16)


NT = (((1,), (1,)), ((), ()))


def gather_sum(mapped, slots):
    r = lax.dot_general(stack(mapped), slots, NT, preferred_element_type=F32)
    n = mapped.shape[0]
    return r[:n] + r[n:]


def kernel(
    curves, groups,
    rhs_ref, start_ref, level_ref, nbr_ref, kind_ref, own0_ref, own1_ref, own2_ref, own3_ref,
    cnbr_ref, ckind_ref, clevel_ref, stiff_ref, smooth_ref, coup_ref, restr_ref,
    out_ref,
    cst, gst, rst, rtst, sst, pk, cnb, ckd, clv, cfield, crow,
    edge_out, from_prev, from_next, part, gpart, hpart,
    esend, erecv, gsend, grecv, hsend, hrecv,
):
    me_c, me_g = lax.axis_index("curve"), lax.axis_index("group")
    me = me_c * groups + me_g
    total = curves * groups
    has_prev, has_next = me > 0, me < total - 1
    prev_id = ((me - 1) // groups, lax.rem(me + groups - 1, groups))
    next_id = ((me + 1) // groups, lax.rem(me + 1, groups))
    kinds_n = coup_ref.shape[0]
    vals = rhs_ref.shape[0]
    per_one = HALF
    per_three = own3_ref.shape[1] // curves
    per_four = cnbr_ref.shape[1] // curves
    ctiles = cfield.shape[0]

    @pl.when(jnp.logical_not(has_prev))
    def _():
        from_prev[...] = jnp.zeros_like(from_prev)

    @pl.when(jnp.logical_not(has_next))
    def _():
        from_next[...] = jnp.zeros_like(from_next)

    start_e, start_i = edge_inner(start_ref)
    edge_out[0] = start_e
    barrier = pltpu.get_barrier_semaphore()

    def greet(where):
        pl.semaphore_signal(barrier, inc=1, device_id=where, device_id_type=MESH)

    @pl.when(has_prev)
    def _():
        greet(prev_id)

    @pl.when(has_next)
    def _():
        greet(next_id)

    def over(count, body):
        if count <= 9:
            for off in range(1, count):
                body(off)
        else:
            def step(off, carry):
                body(off)
                return carry
            lax.fori_loop(1, count, step, 0)

    over(groups, lambda off: greet((me_c, lax.rem(me_g + off, groups))))
    over(curves, lambda off: greet((lax.rem(me_c + off, curves), me_g)))
    pl.semaphore_wait(barrier, groups + curves - 2 + has_prev.astype(jnp.int32) + has_next.astype(jnp.int32))

    def to_prev(r):
        return pltpu.make_async_remote_copy(
            src_ref=edge_out.at[r], dst_ref=from_next.at[r], send_sem=esend.at[r, 0],
            recv_sem=erecv.at[r, 0], device_id=prev_id, device_id_type=MESH)

    def to_next(r):
        return pltpu.make_async_remote_copy(
            src_ref=edge_out.at[r], dst_ref=from_prev.at[r], send_sem=esend.at[r, 1],
            recv_sem=erecv.at[r, 1], device_id=next_id, device_id_type=MESH)

    def send_edges(r):
        @pl.when(has_prev)
        def _():
            to_prev(r).start()

        @pl.when(has_next)
        def _():
            to_next(r).start()

    def halo(r):
        @pl.when(has_next)
        def _():
            to_prev(r).wait_recv()

        @pl.when(has_prev)
        def _():
            to_next(r).wait_recv()

        low = lax.broadcasted_iota(jnp.int32, (vals, LANES), 1) < HALF
        return jnp.where(low, from_next[r], from_prev[r])

    send_edges(0)

    for i in range(cst.shape[1] // LANES):
        two = []
        for t in (2 * i, 2 * i + 1):
            two.append(coup_ref[t] if t < kinds_n else stiff_ref[...] if t == kinds_n else jnp.zeros((vals, vals), F32))
        cst[:, i * LANES:(i + 1) * LANES] = stack(jnp.concatenate(two, axis=1))
    for i in range(rst.shape[1] // LANES):
        one, two = restr_ref[2 * i], restr_ref[2 * i + 1]
        cols = slice(i * LANES, (i + 1) * LANES)
        rst[:, cols] = stack(jnp.concatenate([one, two], axis=1))
        rtst[:, cols] = stack(jnp.concatenate([one.T, two.T], axis=1))
    sst[...] = stack(smooth_ref[...])
    pad = gst.shape[0] - (kinds_n + 1) * vals
    if pad:
        gst[(kinds_n + 1) * vals:, :] = jnp.zeros((pad, 2 * LANES), BF16)

    rhs_e, rhs_i = edge_inner(rhs_ref)
    lev_e, lev_i = edge_inner(level_ref)
    scl_e, scl_i = jnp.exp2(lev_e.astype(F32)), jnp.exp2(lev_i.astype(F32))
    gs_e, gs_i = rhs_e * scl_e, rhs_i * scl_i
    nbr_e, nbr_i = edge_inner(nbr_ref)
    kind_e, kind_i = edge_inner(kind_ref)
    lane8 = lax.broadcasted_iota(jnp.int32, (8, LANES), 1)
    at_i = jnp.where(nbr_i != 0, lane8 + HALF + nbr_i, -1000)
    at_e = jnp.where(nbr_e != 0, jnp.where(lane8 < HALF, lane8, lane8 + LANES) + nbr_e, -1000)
    kind_e = jnp.where(nbr_e != 0, kind_e, -1)
    kind_i = jnp.where(nbr_i != 0, kind_i, -1)

    def couple(own, kinds, picks):
        for k in range(kinds.shape[0]):
            pk[k] = picks(k)

        def one(t):
            acc = jnp.where(kinds[0:1] == t, pk[0], 0.0)
            for k in range(1, kinds.shape[0]):
                acc = acc + jnp.where(kinds[k:k + 1] == t, pk[k], 0.0)
            first = t * vals if isinstance(t, int) else pl.multiple_of(t * vals, vals)
            gst[pl.ds(first, vals), :] = side(acc)

        def body(i, carry):
            one(2 * i)
            one(2 * i + 1)
            return carry

        lax.fori_loop(0, kinds_n // 2, body, 0)
        if kinds_n % 2:
            one(kinds_n - 1)
        gst[kinds_n * vals:(kinds_n + 1) * vals, :] = side(own)
        return fold(jnp.dot(cst[...], gst[...], preferred_element_type=F32))

    def wide(row):
        return jnp.broadcast_to(row, (vals, LANES))

    def inner_image(e, i):
        def picks(k):
            at = wide(at_i[k:k + 1])
            lane = at & (LANES - 1)
            is_inner = (at >= HALF) & (at < HALF + LANES)
            return jnp.where(is_inner, lane_take(i, lane ^ HALF), lane_take(e, lane))
        return couple(i, kind_i, picks)

    def edge_image(e, i, h):
        def picks(k):
            at = wide(at_e[k:k + 1])
            lane = at & (LANES - 1)
            is_inner = (at >= HALF) & (at < HALF + LANES)
            is_own = (at >= 0) & (at < 2 * LANES)
            got = jnp.where(is_own, lane_take(e, lane), lane_take(h, lane))
            return jnp.where(is_inner, lane_take(i, lane ^ HALF), got)
        return couple(e, kind_e, picks)

    def smooth(v, gs, image):
        return v + DAMPING * times(sst[...], gs - image)

    e, i = start_e, start_i
    for r in range(2):
        new_i = smooth(i, gs_i, inner_image(e, i))
        new_e = smooth(e, gs_e, edge_image(e, i, halo(r)))
        e, i = new_e, new_i
        edge_out[r + 1] = e
        send_edges(r + 1)
    res_i = rhs_i - inner_image(e, i) / scl_i
    res_e = rhs_e - edge_image(e, i, halo(2)) / scl_e

    lane_at = lane8
    own0_e, own0_i = edge_inner(own0_ref)
    at_one = jnp.where(lane_at < per_one, me_g * per_one + lane_at, 0)
    par1, oct1 = row_take(own1_ref, 0, at_one), row_take(own1_ref, 1, at_one)
    at_two = jnp.where(lane_at < own2_ref.shape[1], lane_at, 0)
    par2, oct2 = row_take(own2_ref, 0, at_two), row_take(own2_ref, 1, at_two)
    at_three = jnp.where(lane_at < per_three, me_c * per_three + lane_at, 0)
    par3, oct3 = row_take(own3_ref, 0, at_three), row_take(own3_ref, 1, at_three)

    one = (gather_sum(octant_dot(rst[...], res_e, own0_e[1:2]), slots_of(own0_e[0:1]))
           + gather_sum(octant_dot(rst[...], res_i, own0_i[1:2]), slots_of(own0_i[0:1])))
    two = gather_sum(octant_dot(rst[...], one, oct1[0:1]), slots_of(par1[0:1]))
    three = gather_sum(octant_dot(rst[...], two, oct2[0:1]), slots_of(par2[0:1]))
    mapped = octant_dot(rst[...], three, oct3[0:1])
    ids = lax.broadcasted_iota(jnp.int32, (8, LANES), 0)
    slots = jnp.where(ids == par3[0:1], 1.0, 0.0).astype(BF16)
    hi, lo = split(mapped)
    zeros = jnp.zeros_like(hi)
    part[...] = (lax.dot_general(slots, jnp.concatenate([hi, zeros], axis=0), NT, preferred_element_type=F32)
                 + lax.dot_general(slots, jnp.concatenate([lo, zeros], axis=0), NT, preferred_element_type=F32))

    def to_group(off):
        return pltpu.make_async_remote_copy(
            src_ref=part, dst_ref=gpart.at[off], send_sem=gsend.at[off], recv_sem=grecv.at[off],
            device_id=(me_c, lax.rem(me_g + off, groups)), device_id_type=MESH)

    def to_curve(off):
        return pltpu.make_async_remote_copy(
            src_ref=hpart.at[me_c], dst_ref=hpart.at[me_c], send_sem=hsend.at[off], recv_sem=hrecv.at[off],
            device_id=(lax.rem(me_c + off, curves), me_g), device_id_type=MESH)

    def from_curve(off):
        who = lax.rem(me_c + curves - off, curves)
        return pltpu.make_async_remote_copy(
            src_ref=hpart.at[who], dst_ref=hpart.at[who], send_sem=hsend.at[off], recv_sem=hrecv.at[off],
            device_id=(lax.rem(me_c + off, curves), me_g), device_id_type=MESH)

    over(groups, lambda off: to_group(off).start())
    over(groups, lambda off: to_group(off).wait_recv())
    mine = part[...]
    for off in range(1, groups):
        mine = mine + gpart[off]
    hpart[me_c] = mine
    over(curves, lambda off: to_curve(off).start())
    cnb[...] = jnp.full_like(cnb, -1)
    ckd[...] = jnp.full_like(ckd, -1)
    clv[...] = jnp.zeros_like(clv)
    crow[...] = jnp.zeros_like(crow)
    width = cnbr_ref.shape[1]
    cnb[:, :width] = cnbr_ref[...]
    ckd[:, :width] = ckind_ref[...]
    clv[:, :width] = jnp.broadcast_to(clevel_ref[...], (8, width))
    over(curves, lambda off: from_curve(off).wait_recv())

    for m in range(curves):
        crow[m * per_four:(m + 1) * per_four, :] = hpart[m, :per_four, :]
    crhs = []
    for n in range(ctiles):
        cols = slice(n * LANES, (n + 1) * LANES)
        block = crow[cols, :].T[:vals]
        crhs.append(block * jnp.exp2(clv[0:1, cols].astype(F32)))
    field = [DAMPING * times(sst[...], g) for g in crhs]
    for sweep in range(COARSE_SWEEPS - 1):
        new = []
        for n in range(ctiles):
            cols = slice(n * LANES, (n + 1) * LANES)
            at_c = cnb[:, cols]
            kind_c = jnp.where(at_c >= 0, ckd[:, cols], -1)

            def picks(k, at_c=at_c):
                at = wide(at_c[k:k + 1])
                lane = at & (LANES - 1)
                got = lane_take(field[0], lane)
                for s in range(1, ctiles):
                    got = jnp.where((at >> 7) == s, lane_take(field[s], lane), got)
                return got

            new.append(smooth(field[n], crhs[n], couple(field[n], kind_c, picks)))
        field = new

    at = wide(jnp.where(lane_at < per_three, me_c * per_four + par3, 0)[0:1])
    back = lane_take(field[0], at & (LANES - 1))
    for s in range(1, ctiles):
        back = jnp.where((at >> 7) == s, lane_take(field[s], at & (LANES - 1)), back)
    back = octant_dot(rtst[...], back, oct3[0:1])
    back = octant_dot(rtst[...], lane_take(back, wide(par2[0:1])), oct2[0:1])
    back = octant_dot(rtst[...], lane_take(back, wide(par1[0:1])), oct1[0:1])
    e = e + octant_dot(rtst[...], lane_take(back, wide(own0_e[0:1])), own0_e[1:2])
    edge_out[3] = e
    send_edges(3)
    i = i + octant_dot(rtst[...], lane_take(back, wide(own0_i[0:1])), own0_i[1:2])

    new_i = smooth(i, gs_i, inner_image(e, i))
    new_e = smooth(e, gs_e, edge_image(e, i, halo(3)))
    low = lax.broadcasted_iota(jnp.int32, (vals, LANES), 1) < HALF
    turned = swap(new_i)
    out_ref[:, :LANES] = jnp.where(low, new_e, turned)
    out_ref[:, LANES:] = jnp.where(low, turned, new_e)

    over(groups, lambda off: to_group(off).wait_send())
    over(curves, lambda off: to_curve(off).wait_send())

    @pl.when(has_prev)
    def _():
        for r in range(4):
            to_prev(r).wait_send()

    @pl.when(has_next)
    def _():
        for r in range(4):
            to_next(r).wait_send()


def solution(mesh):
    curves, groups = mesh.shape["curve"], mesh.shape["group"]

    def shards(*args):
        args = list(args)
        args[2] = args[2].reshape(1, -1)
        args[11] = args[11].reshape(1, -1)
        rhs, coup, restr = args[0], args[14], args[15]
        vals, blocks = rhs.shape
        kinds = coup.shape[0] + 1
        depth = (kinds + kinds % 2) * vals
        cw = -(-args[9].shape[1] // LANES) * LANES
        rdepth = restr.shape[0] * vals
        assert blocks == 2 * LANES and vals == HALF
        vm = pltpu.VMEM
        return pl.pallas_call(
            functools.partial(kernel, curves, groups),
            out_shape=jax.ShapeDtypeStruct(rhs.shape, F32),
            in_specs=[pl.BlockSpec(memory_space=pltpu.VMEM)] * len(args),
            out_specs=pl.BlockSpec(memory_space=pltpu.VMEM),
            scratch_shapes=[
                vm((2 * vals, depth), BF16),
                vm((depth, 2 * LANES), BF16),
                vm((2 * vals, rdepth), BF16),
                vm((2 * vals, rdepth), BF16),
                vm((2 * vals, vals), BF16),
                vm((8, vals, LANES), F32),
                vm((8, cw), jnp.int32),
                vm((8, cw), jnp.int32),
                vm((8, cw), jnp.int32),
                vm((cw // LANES, vals, LANES), F32),
                vm((cw, LANES), F32),
                vm((4, vals, LANES), F32),
                vm((4, vals, LANES), F32),
                vm((4, vals, LANES), F32),
                vm((8, LANES), F32),
                vm((groups, 8, LANES), F32),
                vm((curves, 8, LANES), F32),
                pltpu.SemaphoreType.DMA((4, 2)),
                pltpu.SemaphoreType.DMA((4, 2)),
                pltpu.SemaphoreType.DMA((groups,)),
                pltpu.SemaphoreType.DMA((groups,)),
                pltpu.SemaphoreType.DMA((curves,)),
                pltpu.SemaphoreType.DMA((curves,)),
            ],
            compiler_params=pltpu.CompilerParams(
                collective_id=0, has_side_effects=True, vmem_limit_bytes=32 * 2**20
            ),
        )(*args)

    fine, part, all_ = P(None, ("curve", "group")), P(None, "curve"), P()
    return jax.shard_map(
        shards,
        mesh=mesh,
        in_specs=(fine, fine, P(("curve", "group")), fine, fine, fine, part, part) + (all_,) * 8,
        out_specs=fine,
        check_vma=False,
    )
```

profile of v0, /device:TPU:1, one launch (start us, length us, event | category | flops | bytes accessed | tf_op | source)
XLA Modules:
  0.0 48.0 jit_solution(14458114647944793495)
XLA Ops:
  0.0 0.0 copy-start.10
  0.0 0.0 copy-start.12
  0.0 0.0 copy-start.15
  0.0 0.7 %copy-done.10 = s32[2,256]{1,0:T(2,128)S(1)} copy-done((s32[2,256]{1,0:T(2,128)S(1)}, s32[2,256]{1,0:T(2,128)}, u32[]{:S(2)}) %copy-start.10) | copy-done | bytes 2072
  0.7 0.0 copy-done.12
  0.7 0.0 copy-done.15
  0.7 0.0 copy-start
  0.7 1.2 %copy-done = f32[30,64,64]{2,1,0:T(8,128)S(1)} copy-done((f32[30,64,64]{2,1,0:T(8,128)S(1)}, f32[30,64,64]{2,1,0:T(8,128)}, u32[]{:S(2)}) %copy-start) | copy-done | bytes 491544
  1.9 0.0 copy-start.1
  1.9 0.9 %copy-done.1 = f32[8,64,64]{2,1,0:T(8,128)S(1)} copy-done((f32[8,64,64]{2,1,0:T(8,128)S(1)}, f32[8,64,64]{2,1,0:T(8,128)}, u32[]{:S(2)}) %copy-start.1) | copy-done | bytes 131096
  2.9 0.0 copy-start.2
  2.9 0.8 %copy-done.2 = f32[64,256]{1,0:T(8,128)S(1)} copy-done((f32[64,256]{1,0:T(8,128)S(1)}, f32[64,256]{1,0:T(8,128)}, u32[]{:S(2)}) %copy-start.2) | copy-done | bytes 65560
  3.7 0.8 %copy-done.3 = f32[64,256]{1,0:T(8,128)S(1)} copy-done((f32[64,256]{1,0:T(8,128)S(1)}, f32[64,256]{1,0:T(8,128)}, u32[]{:S(2)}) %copy-start.3) | copy-done | bytes 65560
  4.5 0.8 %copy-done.4 = f32[64,64]{1,0:T(8,128)S(1)} copy-done((f32[64,64]{1,0:T(8,128)S(1)}, f32[64,64]{1,0:T(8,128)}, u32[]{:S(2)}) %copy-start.4) | copy-done | bytes 16408
  5.3 0.8 %copy-done.5 = f32[64,64]{1,0:T(8,128)S(1)} copy-done((f32[64,64]{1,0:T(8,128)S(1)}, f32[64,64]{1,0:T(8,128)}, u32[]{:S(2)}) %copy-start.5) | copy-done | bytes 16408
  6.1 0.7 %copy-done.6 = s32[8,256]{1,0:T(8,128)S(1)} copy-done((s32[8,256]{1,0:T(8,128)S(1)}, s32[8,256]{1,0:T(8,128)}, u32[]{:S(2)}) %copy-start.6) | copy-done | bytes 8216
  6.7 0.7 %copy-done.7 = s32[8,256]{1,0:T(8,128)S(1)} copy-done((s32[8,256]{1,0:T(8,128)S(1)}, s32[8,256]{1,0:T(8,128)}, u32[]{:S(2)}) %copy-start.7) | copy-done | bytes 8216
  7.4 0.7 %copy-done.8 = s32[8,32]{1,0:T(8,128)S(1)} copy-done((s32[8,32]{1,0:T(8,128)S(1)}, s32[8,32]{1,0:T(8,128)}, u32[]{:S(2)}) %copy-start.8) | copy-done | bytes 1048
  8.1 0.7 %copy-done.9 = s32[8,32]{1,0:T(8,128)S(1)} copy-done((s32[8,32]{1,0:T(8,128)S(1)}, s32[8,32]{1,0:T(8,128)}, u32[]{:S(2)}) %copy-start.9) | copy-done | bytes 1048
  8.8 0.7 %copy-done.11 = s32[2,256]{1,0:T(2,128)S(1)} copy-done((s32[2,256]{1,0:T(2,128)S(1)}, s32[2,256]{1,0:T(2,128)}, u32[]{:S(2)}) %copy-start.11) | copy-done | bytes 2072
  9.5 0.7 %copy-done.13 = s32[2,64]{1,0:T(2,128)S(1)} copy-done((s32[2,64]{1,0:T(2,128)S(1)}, s32[2,64]{1,0:T(2,128)}, u32[]{:S(2)}) %copy-start.13) | copy-done | bytes 536
  10.2 0.7 %copy-done.14 = s32[2,128]{1,0:T(2,128)S(1)} copy-done((s32[2,128]{1,0:T(2,128)S(1)}, s32[2,128]{1,0:T(2,128)}, u32[]{:S(2)}) %copy-start.14) | copy-done | bytes 1048
  10.9 36.5 %shard_map.154 = f32[64,256]{1,0:T(8,128)S(1)} custom-call(f32[64,256]{1,0:T(8,128)S(1)} %copy-done.2, f32[64,256]{1,0:T(8,128)S(1)} %copy-done.3, s32[1,256]{1,0:T(1,128)S(1)} %bitcast.2, s32[8,256]{1,0:T(8,128)S(1)} %copy-done.6, s32[8,256]{1,0:T(8,128)S(1)} %copy-done.7, s32[2,256]{1,0:T(2,128)S(1)} %copy-done.10, s32[2,256]{1,0:T(2,128)S(1)} %copy-done.11, ...), custom_call_target="tpu_custom_call" | custom-call | tf_op jit(solution)/shard_map/pallas_call | solution.py:390
  47.3 0.6 %copy.18 = f32[64,256]{1,0:T(8,128)} copy(f32[64,256]{1,0:T(8,128)S(1)} %shard_map.154) | data formatting | bytes 131072
  (10 shorter events, 0.0 us)
Async XLA Ops:
  0.0 0.7 %copy-start.10 = (s32[2,256]{1,0:T(2,128)S(1)}, s32[2,256]{1,0:T(2,128)}, u32[]{:S(2)}) copy-start(s32[2,256]{1,0:T(2,128)} %own0_ref.1) | copy-start | bytes 6148
  0.0 0.7 %copy-start.12 = (s32[256]{0:T(256)S(1)}, s32[256]{0:T(256)}, u32[]{:S(2)}) copy-start(s32[256]{0:T(256)} %param.18) | copy-start | bytes 3076
  0.0 0.7 %copy-start.15 = (s32[32]{0:T(128)S(1)}, s32[32]{0:T(128)}, u32[]{:S(2)}) copy-start(s32[32]{0:T(128)} %param.27) | copy-start | bytes 388
  0.7 1.2 %copy-start = (f32[30,64,64]{2,1,0:T(8,128)S(1)}, f32[30,64,64]{2,1,0:T(8,128)}, u32[]{:S(2)}) copy-start(f32[30,64,64]{2,1,0:T(8,128)} %coup_ref.1) | copy-start | bytes 1474564
  1.9 0.9 %copy-start.1 = (f32[8,64,64]{2,1,0:T(8,128)S(1)}, f32[8,64,64]{2,1,0:T(8,128)}, u32[]{:S(2)}) copy-start(f32[8,64,64]{2,1,0:T(8,128)} %restr_ref.1) | copy-start | bytes 393220
  2.9 0.8 %copy-start.2 = (f32[64,256]{1,0:T(8,128)S(1)}, f32[64,256]{1,0:T(8,128)}, u32[]{:S(2)}) copy-start(f32[64,256]{1,0:T(8,128)} %rhs_ref.1) | copy-start | bytes 196612
  3.7 0.8 %copy-start.3 = (f32[64,256]{1,0:T(8,128)S(1)}, f32[64,256]{1,0:T(8,128)}, u32[]{:S(2)}) copy-start(f32[64,256]{1,0:T(8,128)} %start_ref.1) | copy-start | bytes 196612
  4.5 0.8 %copy-start.4 = (f32[64,64]{1,0:T(8,128)S(1)}, f32[64,64]{1,0:T(8,128)}, u32[]{:S(2)}) copy-start(f32[64,64]{1,0:T(8,128)} %stiff_ref.1) | copy-start | bytes 49156
  5.3 0.8 %copy-start.5 = (f32[64,64]{1,0:T(8,128)S(1)}, f32[64,64]{1,0:T(8,128)}, u32[]{:S(2)}) copy-start(f32[64,64]{1,0:T(8,128)} %smooth_ref.1) | copy-start | bytes 49156
  6.0 0.7 %copy-start.6 = (s32[8,256]{1,0:T(8,128)S(1)}, s32[8,256]{1,0:T(8,128)}, u32[]{:S(2)}) copy-start(s32[8,256]{1,0:T(8,128)} %nbr_ref.1) | copy-start | bytes 24580
  6.7 0.7 %copy-start.7 = (s32[8,256]{1,0:T(8,128)S(1)}, s32[8,256]{1,0:T(8,128)}, u32[]{:S(2)}) copy-start(s32[8,256]{1,0:T(8,128)} %kind_ref.1) | copy-start | bytes 24580
  7.4 0.7 %copy-start.8 = (s32[8,32]{1,0:T(8,128)S(1)}, s32[8,32]{1,0:T(8,128)}, u32[]{:S(2)}) copy-start(s32[8,32]{1,0:T(8,128)} %cnbr_ref.1) | copy-start | bytes 3076
  8.1 0.7 %copy-start.9 = (s32[8,32]{1,0:T(8,128)S(1)}, s32[8,32]{1,0:T(8,128)}, u32[]{:S(2)}) copy-start(s32[8,32]{1,0:T(8,128)} %ckind_ref.1) | copy-start | bytes 3076
  8.8 0.7 %copy-start.11 = (s32[2,256]{1,0:T(2,128)S(1)}, s32[2,256]{1,0:T(2,128)}, u32[]{:S(2)}) copy-start(s32[2,256]{1,0:T(2,128)} %own1_ref.1) | copy-start | bytes 6148
  9.5 0.7 %copy-start.13 = (s32[2,64]{1,0:T(2,128)S(1)}, s32[2,64]{1,0:T(2,128)}, u32[]{:S(2)}) copy-start(s32[2,64]{1,0:T(2,128)} %own2_ref.1) | copy-start | bytes 1540
  10.2 0.7 %copy-start.14 = (s32[2,128]{1,0:T(2,128)S(1)}, s32[2,128]{1,0:T(2,128)}, u32[]{:S(2)}) copy-start(s32[2,128]{1,0:T(2,128)} %own3_ref.1) | copy-start | bytes 3076
where the time goes:
time: 48.6 us; the launch traced here: 48 us
  Pallas kernels  36.5 us (75%)
  local copies, waits for them, and re-layouts  11.5 us (24%)
    pallas_call x1, Pallas kernels, shards(): pl.pallas_call(functools.partial(kernel, curves, groups), out_shape=jax.S...  36.5 us
    unnamed x33, local copies, waits for them, and re-layouts  11.5 us

commit v1 on v0

--- a/solution.py
+++ b/solution.py
@@ -66,8 +66,13 @@
 
 
 def octant_dot(left, x, octant):
-    parts = [jnp.where(octant == o, x, 0.0) for o in range(left.shape[1] // x.shape[0])]
-    return times(left, jnp.concatenate(parts, axis=0))
+    n = x.shape[0]
+    whole = stack(x)
+    code = jnp.broadcast_to(octant.astype(F32), whole.shape).astype(BF16)
+    parts = [jnp.where(code == jnp.asarray(o, BF16), whole, jnp.zeros_like(whole)) for o in range(left.shape[1] // n)]
+    high = jnp.concatenate([p[:n] for p in parts], axis=0)
+    low = jnp.concatenate([p[n:] for p in parts], axis=0)
+    return fold(jnp.dot(left, jnp.concatenate([high, low], axis=1), preferred_element_type=F32))
 
 
 def slots_of(parent):
@@ -85,11 +90,21 @@
 
 
 def kernel(
-    curves, groups,
+    curves, groups, n_in, *refs
+):
+    held, done = refs[n_in + 1:2 * n_in + 1], refs[2 * n_in + 1]
+    loads = [pltpu.make_async_copy(refs[n], held[n], done.at[n]) for n in range(n_in)]
+    for n in (1, 0) + tuple(range(2, n_in)):
+        loads[n].start()
+    cycle(curves, groups, loads, *held, refs[n_in], *refs[2 * n_in + 2:])
+
+
+def cycle(
+    curves, groups, loads,
     rhs_ref, start_ref, level_ref, nbr_ref, kind_ref, own0_ref, own1_ref, own2_ref, own3_ref,
     cnbr_ref, ckind_ref, clevel_ref, stiff_ref, smooth_ref, coup_ref, restr_ref,
     out_ref,
-    cst, gst, rst, rtst, sst, pk, cnb, ckd, clv, cfield, crow,
+    cst, mst, gst, rst, rtst, sst, cnb, ckd, clv, cfield, crow,
     edge_out, from_prev, from_next, part, gpart, hpart,
     esend, erecv, gsend, grecv, hsend, hrecv,
 ):
@@ -114,8 +129,6 @@
     def _():
         from_next[...] = jnp.zeros_like(from_next)
 
-    start_e, start_i = edge_inner(start_ref)
-    edge_out[0] = start_e
     barrier = pltpu.get_barrier_semaphore()
 
     def greet(where):
@@ -141,6 +154,9 @@
 
     over(groups, lambda off: greet((me_c, lax.rem(me_g + off, groups))))
     over(curves, lambda off: greet((lax.rem(me_c + off, curves), me_g)))
+    loads[1].wait()
+    start_e, start_i = edge_inner(start_ref)
+    edge_out[0] = start_e
     pl.semaphore_wait(barrier, groups + curves - 2 + has_prev.astype(jnp.int32) + has_next.astype(jnp.int32))
 
     def to_prev(r):
@@ -175,18 +191,23 @@
         return jnp.where(low, from_next[r], from_prev[r])
 
     send_edges(0)
-
+    for n, load in enumerate(loads):
+        if n != 1:
+            load.wait()
+
+    sst[...] = stack(DAMPING * smooth_ref[...])
     for i in range(cst.shape[1] // LANES):
         two = []
         for t in (2 * i, 2 * i + 1):
             two.append(coup_ref[t] if t < kinds_n else stiff_ref[...] if t == kinds_n else jnp.zeros((vals, vals), F32))
-        cst[:, i * LANES:(i + 1) * LANES] = stack(jnp.concatenate(two, axis=1))
+        both = jnp.concatenate(two, axis=1)
+        cst[:, i * LANES:(i + 1) * LANES] = stack(both)
+        mst[:, i * LANES:(i + 1) * LANES] = stack(times(sst[...], both))
     for i in range(rst.shape[1] // LANES):
         one, two = restr_ref[2 * i], restr_ref[2 * i + 1]
         cols = slice(i * LANES, (i + 1) * LANES)
         rst[:, cols] = stack(jnp.concatenate([one, two], axis=1))
         rtst[:, cols] = stack(jnp.concatenate([one.T, two.T], axis=1))
-    sst[...] = stack(smooth_ref[...])
     pad = gst.shape[0] - (kinds_n + 1) * vals
     if pad:
         gst[(kinds_n + 1) * vals:, :] = jnp.zeros((pad, 2 * LANES), BF16)
@@ -203,40 +224,38 @@
     kind_e = jnp.where(nbr_e != 0, kind_e, -1)
     kind_i = jnp.where(nbr_i != 0, kind_i, -1)
 
-    def couple(own, kinds, picks):
-        for k in range(kinds.shape[0]):
-            pk[k] = picks(k)
-
-        def one(t):
-            acc = jnp.where(kinds[0:1] == t, pk[0], 0.0)
-            for k in range(1, kinds.shape[0]):
-                acc = acc + jnp.where(kinds[k:k + 1] == t, pk[k], 0.0)
-            first = t * vals if isinstance(t, int) else pl.multiple_of(t * vals, vals)
-            gst[pl.ds(first, vals), :] = side(acc)
-
-        def body(i, carry):
-            one(2 * i)
-            one(2 * i + 1)
-            return carry
-
-        lax.fori_loop(0, kinds_n // 2, body, 0)
-        if kinds_n % 2:
-            one(kinds_n - 1)
+    def couple(left, own, kinds, picks):
+        slots_n = kinds.shape[0]
+        picked = [picks(k) for k in range(slots_n)]
+        codes, parts = [], []
+        for k in range(slots_n):
+            whole = picked[k]
+            for other in range(k):
+                same = kinds[other:other + 1] == kinds[k:k + 1]
+                whole = whole + jnp.where(same, picked[other], 0.0)
+            parts.append(stack(whole))
+            codes.append(jnp.broadcast_to(kinds[k:k + 1].astype(F32), (2 * vals, LANES)).astype(BF16))
+        for t in range(kinds_n):
+            acc = jnp.zeros_like(parts[0])
+            for k in range(slots_n):
+                acc = jnp.where(codes[k] == jnp.asarray(t, BF16), parts[k], acc)
+            gst[t * vals:(t + 1) * vals, :LANES] = acc[:vals]
+            gst[t * vals:(t + 1) * vals, LANES:] = acc[vals:]
         gst[kinds_n * vals:(kinds_n + 1) * vals, :] = side(own)
-        return fold(jnp.dot(cst[...], gst[...], preferred_element_type=F32))
+        return fold(jnp.dot(left[...], gst[...], preferred_element_type=F32))
 
     def wide(row):
         return jnp.broadcast_to(row, (vals, LANES))
 
-    def inner_image(e, i):
+    def inner_image(left, e, i):
         def picks(k):
             at = wide(at_i[k:k + 1])
             lane = at & (LANES - 1)
             is_inner = (at >= HALF) & (at < HALF + LANES)
             return jnp.where(is_inner, lane_take(i, lane ^ HALF), lane_take(e, lane))
-        return couple(i, kind_i, picks)
-
-    def edge_image(e, i, h):
+        return couple(left, i, kind_i, picks)
+
+    def edge_image(left, e, i, h):
         def picks(k):
             at = wide(at_e[k:k + 1])
             lane = at & (LANES - 1)
@@ -244,20 +263,22 @@
             is_own = (at >= 0) & (at < 2 * LANES)
             got = jnp.where(is_own, lane_take(e, lane), lane_take(h, lane))
             return jnp.where(is_inner, lane_take(i, lane ^ HALF), got)
-        return couple(e, kind_e, picks)
-
-    def smooth(v, gs, image):
-        return v + DAMPING * times(sst[...], gs - image)
+        return couple(left, e, kind_e, picks)
+
+    def smooth(v, moved, image):
+        return v + (moved - image)
+
+    gs_e, gs_i = times(sst[...], gs_e), times(sst[...], gs_i)
 
     e, i = start_e, start_i
     for r in range(2):
-        new_i = smooth(i, gs_i, inner_image(e, i))
-        new_e = smooth(e, gs_e, edge_image(e, i, halo(r)))
+        new_i = smooth(i, gs_i, inner_image(mst, e, i))
+        new_e = smooth(e, gs_e, edge_image(mst, e, i, halo(r)))
         e, i = new_e, new_i
         edge_out[r + 1] = e
         send_edges(r + 1)
-    res_i = rhs_i - inner_image(e, i) / scl_i
-    res_e = rhs_e - edge_image(e, i, halo(2)) / scl_e
+    res_i = rhs_i - inner_image(cst, e, i) / scl_i
+    res_e = rhs_e - edge_image(cst, e, i, halo(2)) / scl_e
 
     lane_at = lane8
     own0_e, own0_i = edge_inner(own0_ref)
@@ -319,8 +340,8 @@
     for n in range(ctiles):
         cols = slice(n * LANES, (n + 1) * LANES)
         block = crow[cols, :].T[:vals]
-        crhs.append(block * jnp.exp2(clv[0:1, cols].astype(F32)))
-    field = [DAMPING * times(sst[...], g) for g in crhs]
+        crhs.append(times(sst[...], block * jnp.exp2(clv[0:1, cols].astype(F32))))
+    field = crhs
     for sweep in range(COARSE_SWEEPS - 1):
         new = []
         for n in range(ctiles):
@@ -336,7 +357,7 @@
                     got = jnp.where((at >> 7) == s, lane_take(field[s], lane), got)
                 return got
 
-            new.append(smooth(field[n], crhs[n], couple(field[n], kind_c, picks)))
+            new.append(smooth(field[n], crhs[n], couple(mst, field[n], kind_c, picks)))
         field = new
 
     at = wide(jnp.where(lane_at < per_three, me_c * per_four + par3, 0)[0:1])
@@ -351,8 +372,8 @@
     send_edges(3)
     i = i + octant_dot(rtst[...], lane_take(back, wide(own0_i[0:1])), own0_i[1:2])
 
-    new_i = smooth(i, gs_i, inner_image(e, i))
-    new_e = smooth(e, gs_e, edge_image(e, i, halo(3)))
+    new_i = smooth(i, gs_i, inner_image(mst, e, i))
+    new_e = smooth(e, gs_e, edge_image(mst, e, i, halo(3)))
     low = lax.broadcasted_iota(jnp.int32, (vals, LANES), 1) < HALF
     turned = swap(new_i)
     out_ref[:, :LANES] = jnp.where(low, new_e, turned)
@@ -388,17 +409,18 @@
         assert blocks == 2 * LANES and vals == HALF
         vm = pltpu.VMEM
         return pl.pallas_call(
-            functools.partial(kernel, curves, groups),
+            functools.partial(kernel, curves, groups, len(args)),
             out_shape=jax.ShapeDtypeStruct(rhs.shape, F32),
-            in_specs=[pl.BlockSpec(memory_space=pltpu.VMEM)] * len(args),
+            in_specs=[pl.BlockSpec(memory_space=pltpu.HBM)] * len(args),
             out_specs=pl.BlockSpec(memory_space=pltpu.VMEM),
-            scratch_shapes=[
+            scratch_shapes=[vm(a.shape, a.dtype) for a in args] + [
+                pltpu.SemaphoreType.DMA((len(args),)),
+                vm((2 * vals, depth), BF16),
                 vm((2 * vals, depth), BF16),
                 vm((depth, 2 * LANES), BF16),
                 vm((2 * vals, rdepth), BF16),
                 vm((2 * vals, rdepth), BF16),
                 vm((2 * vals, vals), BF16),
-                vm((8, vals, LANES), F32),
                 vm((8, cw), jnp.int32),
                 vm((8, cw), jnp.int32),
                 vm((8, cw), jnp.int32),
@@ -418,7 +440,7 @@
                 pltpu.SemaphoreType.DMA((curves,)),
             ],
             compiler_params=pltpu.CompilerParams(
-                collective_id=0, has_side_effects=True, vmem_limit_bytes=32 * 2**20
+                collective_id=0, has_side_effects=True, vmem_limit_bytes=60 * 2**20
             ),
         )(*args)
 

time: 48.6 us -> 35.8 us (0.74)
  local copies, waits for them, and re-layouts: 11.5 us -> 1.47 us
  Pallas kernels: 36.5 us -> 34.1 us
    unnamed x33 -> x1, local copies, waits for them, and re-layouts: 11.5 us -> 1.47 us
    pallas_call x1, Pallas kernels: 36.5 us -> 34.1 us  [shards(): pl.pallas_call(functools.partial(kernel, curves, groups, len(args)), out_...]
where the time goes in v1:
time: 35.8 us; the launch traced here: 35.6 us
  Pallas kernels  34.1 us (95%)
  local copies, waits for them, and re-layouts  1.47 us (4%)
    pallas_call x1, Pallas kernels, shards(): pl.pallas_call(functools.partial(kernel, curves, groups, len(args)), out_...  34.1 us
    unnamed x1, local copies, waits for them, and re-layouts  1.47 us

profile of v1, /device:TPU:1, one launch (start us, length us, event | category | flops | bytes accessed | tf_op | source)
XLA Modules:
  0.0 35.6 jit_solution(1679652544600232094)
XLA Ops:
  0.0 34.1 %shard_map.154 = f32[64,256]{1,0:T(8,128)} custom-call(f32[64,256]{1,0:T(8,128)} %refs_0_.1, f32[64,256]{1,0:T(8,128)} %refs_1_.1, s32[1,256]{1,0:T(1,128)} %bitcast.2, s32[8,256]{1,0:T(8,128)} %refs_3_.1, s32[8,256]{1,0:T(8,128)} %refs_4_.1, s32[2,256]{1,0:T(2,128)} %refs_5_.1, s32[2,256]{1,0:T(2,128)} %refs_6_.1, s32[2,64]{1,0:T(2,128)} %refs_7_.1, ...), custom_call_target="tpu_custom_call" | custom-call | tf_op jit(solution)/shard_map/pallas_call | solution.py:411
  34.2 1.5 %copy.18 = f32[64,256]{1,0:T(8,128)} copy(f32[64,256]{1,0:T(8,128)} %shard_map.154) | data formatting | bytes 131072

commit v2 on v1

--- a/solution.py
+++ b/solution.py
@@ -92,19 +92,19 @@
 def kernel(
     curves, groups, n_in, *refs
 ):
-    held, done = refs[n_in + 1:2 * n_in + 1], refs[2 * n_in + 1]
+    held, done = refs[n_in + 2:2 * n_in + 2], refs[2 * n_in + 2]
     loads = [pltpu.make_async_copy(refs[n], held[n], done.at[n]) for n in range(n_in)]
     for n in (1, 0) + tuple(range(2, n_in)):
         loads[n].start()
-    cycle(curves, groups, loads, *held, refs[n_in], *refs[2 * n_in + 2:])
+    cycle(curves, groups, loads, *held, *refs[n_in:n_in + 2], *refs[2 * n_in + 3:])
 
 
 def cycle(
     curves, groups, loads,
     rhs_ref, start_ref, level_ref, nbr_ref, kind_ref, own0_ref, own1_ref, own2_ref, own3_ref,
     cnbr_ref, ckind_ref, clevel_ref, stiff_ref, smooth_ref, coup_ref, restr_ref,
-    out_ref,
-    cst, mst, gst, rst, rtst, sst, cnb, ckd, clv, cfield, crow,
+    base_ref, step_ref,
+    mats, gst, rst, rtst, sst, cnb, ckd, clv, cfield, crhs, crow, cur, res, fix,
     edge_out, from_prev, from_next, part, gpart, hpart,
     esend, erecv, gsend, grecv, hsend, hrecv,
 ):
@@ -119,7 +119,7 @@
     per_one = HALF
     per_three = own3_ref.shape[1] // curves
     per_four = cnbr_ref.shape[1] // curves
-    ctiles = cfield.shape[0]
+    ctiles = cfield.shape[1]
 
     @pl.when(jnp.logical_not(has_prev))
     def _():
@@ -196,13 +196,13 @@
             load.wait()
 
     sst[...] = stack(DAMPING * smooth_ref[...])
-    for i in range(cst.shape[1] // LANES):
+    for i in range(mats.shape[2] // LANES):
         two = []
         for t in (2 * i, 2 * i + 1):
             two.append(coup_ref[t] if t < kinds_n else stiff_ref[...] if t == kinds_n else jnp.zeros((vals, vals), F32))
         both = jnp.concatenate(two, axis=1)
-        cst[:, i * LANES:(i + 1) * LANES] = stack(both)
-        mst[:, i * LANES:(i + 1) * LANES] = stack(times(sst[...], both))
+        mats[1, :, i * LANES:(i + 1) * LANES] = stack(both)
+        mats[0, :, i * LANES:(i + 1) * LANES] = stack(times(sst[...], both))
     for i in range(rst.shape[1] // LANES):
         one, two = restr_ref[2 * i], restr_ref[2 * i + 1]
         cols = slice(i * LANES, (i + 1) * LANES)
@@ -265,20 +265,11 @@
             return jnp.where(is_inner, lane_take(i, lane ^ HALF), got)
         return couple(left, e, kind_e, picks)
 
-    def smooth(v, moved, image):
-        return v + (moved - image)
-
-    gs_e, gs_i = times(sst[...], gs_e), times(sst[...], gs_i)
-
-    e, i = start_e, start_i
-    for r in range(2):
-        new_i = smooth(i, gs_i, inner_image(mst, e, i))
-        new_e = smooth(e, gs_e, edge_image(mst, e, i, halo(r)))
-        e, i = new_e, new_i
-        edge_out[r + 1] = e
-        send_edges(r + 1)
-    res_i = rhs_i - inner_image(cst, e, i) / scl_i
-    res_e = rhs_e - edge_image(cst, e, i, halo(2)) / scl_e
+    fix[0, 0], fix[0, 1] = times(sst[...], gs_e), times(sst[...], gs_i)
+    fix[1, 0], fix[1, 1] = rhs_e, rhs_i
+    fix[2, 0] = jnp.broadcast_to(1.0 / scl_e, (vals, LANES))
+    fix[2, 1] = jnp.broadcast_to(1.0 / scl_i, (vals, LANES))
+    cur[0], cur[1] = start_e, start_i
 
     lane_at = lane8
     own0_e, own0_i = edge_inner(own0_ref)
@@ -289,17 +280,17 @@
     at_three = jnp.where(lane_at < per_three, me_c * per_three + lane_at, 0)
     par3, oct3 = row_take(own3_ref, 0, at_three), row_take(own3_ref, 1, at_three)
 
-    one = (gather_sum(octant_dot(rst[...], res_e, own0_e[1:2]), slots_of(own0_e[0:1]))
-           + gather_sum(octant_dot(rst[...], res_i, own0_i[1:2]), slots_of(own0_i[0:1])))
-    two = gather_sum(octant_dot(rst[...], one, oct1[0:1]), slots_of(par1[0:1]))
-    three = gather_sum(octant_dot(rst[...], two, oct2[0:1]), slots_of(par2[0:1]))
-    mapped = octant_dot(rst[...], three, oct3[0:1])
-    ids = lax.broadcasted_iota(jnp.int32, (8, LANES), 0)
-    slots = jnp.where(ids == par3[0:1], 1.0, 0.0).astype(BF16)
-    hi, lo = split(mapped)
-    zeros = jnp.zeros_like(hi)
-    part[...] = (lax.dot_general(slots, jnp.concatenate([hi, zeros], axis=0), NT, preferred_element_type=F32)
-                 + lax.dot_general(slots, jnp.concatenate([lo, zeros], axis=0), NT, preferred_element_type=F32))
+    width = cnbr_ref.shape[1]
+    cnb[...] = jnp.full_like(cnb, -1)
+    ckd[...] = jnp.full_like(ckd, -1)
+    clv[...] = jnp.zeros_like(clv)
+    crow[...] = jnp.zeros_like(crow)
+    for n in range(ctiles):
+        size = min(LANES, width - n * LANES)
+        cols = slice(n * LANES, n * LANES + size)
+        cnb[n, :, :size] = cnbr_ref[:, cols]
+        ckd[n, :, :size] = ckind_ref[:, cols]
+        clv[n, :, :size] = jnp.broadcast_to(clevel_ref[:, cols], (8, size))
 
     def to_group(off):
         return pltpu.make_async_remote_copy(
@@ -317,67 +308,103 @@
             src_ref=hpart.at[who], dst_ref=hpart.at[who], send_sem=hsend.at[off], recv_sem=hrecv.at[off],
             device_id=(lax.rem(me_c + off, curves), me_g), device_id_type=MESH)
 
-    over(groups, lambda off: to_group(off).start())
-    over(groups, lambda off: to_group(off).wait_recv())
-    mine = part[...]
-    for off in range(1, groups):
-        mine = mine + gpart[off]
-    hpart[me_c] = mine
-    over(curves, lambda off: to_curve(off).start())
-    cnb[...] = jnp.full_like(cnb, -1)
-    ckd[...] = jnp.full_like(ckd, -1)
-    clv[...] = jnp.zeros_like(clv)
-    crow[...] = jnp.zeros_like(crow)
-    width = cnbr_ref.shape[1]
-    cnb[:, :width] = cnbr_ref[...]
-    ckd[:, :width] = ckind_ref[...]
-    clv[:, :width] = jnp.broadcast_to(clevel_ref[...], (8, width))
-    over(curves, lambda off: from_curve(off).wait_recv())
-
-    for m in range(curves):
-        crow[m * per_four:(m + 1) * per_four, :] = hpart[m, :per_four, :]
-    crhs = []
-    for n in range(ctiles):
-        cols = slice(n * LANES, (n + 1) * LANES)
-        block = crow[cols, :].T[:vals]
-        crhs.append(times(sst[...], block * jnp.exp2(clv[0:1, cols].astype(F32))))
-    field = crhs
-    for sweep in range(COARSE_SWEEPS - 1):
-        new = []
+    def middle():
+        one = (gather_sum(octant_dot(rst[...], res[0], own0_e[1:2]), slots_of(own0_e[0:1]))
+               + gather_sum(octant_dot(rst[...], res[1], own0_i[1:2]), slots_of(own0_i[0:1])))
+        two = gather_sum(octant_dot(rst[...], one, oct1[0:1]), slots_of(par1[0:1]))
+        three = gather_sum(octant_dot(rst[...], two, oct2[0:1]), slots_of(par2[0:1]))
+        mapped = octant_dot(rst[...], three, oct3[0:1])
+        ids = lax.broadcasted_iota(jnp.int32, (8, LANES), 0)
+        slots = jnp.where(ids == par3[0:1], 1.0, 0.0).astype(BF16)
+        hi, lo = split(mapped)
+        zeros = jnp.zeros_like(hi)
+        part[...] = (lax.dot_general(slots, jnp.concatenate([hi, zeros], axis=0), NT, preferred_element_type=F32)
+                     + lax.dot_general(slots, jnp.concatenate([lo, zeros], axis=0), NT, preferred_element_type=F32))
+
+        over(groups, lambda off: to_group(off).start())
+        over(groups, lambda off: to_group(off).wait_recv())
+        mine = part[...]
+        for off in range(1, groups):
+            mine = mine + gpart[off]
+        hpart[me_c] = mine
+        over(curves, lambda off: to_curve(off).start())
+        over(curves, lambda off: from_curve(off).wait_recv())
+
+        for m in range(curves):
+            crow[m * per_four:(m + 1) * per_four, :] = hpart[m, :per_four, :]
         for n in range(ctiles):
-            cols = slice(n * LANES, (n + 1) * LANES)
-            at_c = cnb[:, cols]
-            kind_c = jnp.where(at_c >= 0, ckd[:, cols], -1)
-
-            def picks(k, at_c=at_c):
+            block = crow[n * LANES:(n + 1) * LANES, :].T[:vals]
+            crhs[n] = times(sst[...], block * jnp.exp2(clv[n, 0:1].astype(F32)))
+            cfield[0, n] = crhs[n]
+
+        def coarse_step(s, carry):
+            sweep, n = s // ctiles, lax.rem(s, ctiles)
+            old = lax.rem(sweep, 2)
+            at_c = cnb[n]
+            kind_c = jnp.where(at_c >= 0, ckd[n], -1)
+            field = [cfield[old, m] for m in range(ctiles)]
+            own = cfield[old, n]
+
+            def picks(k):
                 at = wide(at_c[k:k + 1])
                 lane = at & (LANES - 1)
                 got = lane_take(field[0], lane)
-                for s in range(1, ctiles):
-                    got = jnp.where((at >> 7) == s, lane_take(field[s], lane), got)
+                for m in range(1, ctiles):
+                    got = jnp.where((at >> 7) == m, lane_take(field[m], lane), got)
                 return got
 
-            new.append(smooth(field[n], crhs[n], couple(mst, field[n], kind_c, picks)))
-        field = new
-
-    at = wide(jnp.where(lane_at < per_three, me_c * per_four + par3, 0)[0:1])
-    back = lane_take(field[0], at & (LANES - 1))
-    for s in range(1, ctiles):
-        back = jnp.where((at >> 7) == s, lane_take(field[s], at & (LANES - 1)), back)
-    back = octant_dot(rtst[...], back, oct3[0:1])
-    back = octant_dot(rtst[...], lane_take(back, wide(par2[0:1])), oct2[0:1])
-    back = octant_dot(rtst[...], lane_take(back, wide(par1[0:1])), oct1[0:1])
-    e = e + octant_dot(rtst[...], lane_take(back, wide(own0_e[0:1])), own0_e[1:2])
-    edge_out[3] = e
-    send_edges(3)
-    i = i + octant_dot(rtst[...], lane_take(back, wide(own0_i[0:1])), own0_i[1:2])
-
-    new_i = smooth(i, gs_i, inner_image(mst, e, i))
-    new_e = smooth(e, gs_e, edge_image(mst, e, i, halo(3)))
-    low = lax.broadcasted_iota(jnp.int32, (vals, LANES), 1) < HALF
-    turned = swap(new_i)
-    out_ref[:, :LANES] = jnp.where(low, new_e, turned)
-    out_ref[:, LANES:] = jnp.where(low, turned, new_e)
+            cfield[1 - old, n] = own + (crhs[n] - couple(mats.at[0], own, kind_c, picks))
+            return carry
+
+        lax.fori_loop(0, (COARSE_SWEEPS - 1) * ctiles, coarse_step, 0)
+        field = [cfield[(COARSE_SWEEPS - 1) % 2, m] for m in range(ctiles)]
+
+        at = wide(jnp.where(lane_at < per_three, me_c * per_four + par3, 0)[0:1])
+        back = lane_take(field[0], at & (LANES - 1))
+        for s in range(1, ctiles):
+            back = jnp.where((at >> 7) == s, lane_take(field[s], at & (LANES - 1)), back)
+        back = octant_dot(rtst[...], back, oct3[0:1])
+        back = octant_dot(rtst[...], lane_take(back, wide(par2[0:1])), oct2[0:1])
+        back = octant_dot(rtst[...], lane_take(back, wide(par1[0:1])), oct1[0:1])
+        e = cur[0] + octant_dot(rtst[...], lane_take(back, wide(own0_e[0:1])), own0_e[1:2])
+        edge_out[3] = e
+        cur[0] = e
+        send_edges(3)
+        cur[1] = cur[1] + octant_dot(rtst[...], lane_take(back, wide(own0_i[0:1])), own0_i[1:2])
+
+    def sweep(r, carry):
+        @pl.when(r == 3)
+        def _():
+            middle()
+
+        left = mats.at[(r == 2).astype(jnp.int32)]
+        inner = inner_image(left, cur[0], cur[1])
+        edge = edge_image(left, cur[0], cur[1], halo(r))
+
+        @pl.when(r == 2)
+        def _():
+            res[0] = fix[1, 0] - edge * fix[2, 0]
+            res[1] = fix[1, 1] - inner * fix[2, 1]
+
+        @pl.when(r < 2)
+        def _():
+            new = cur[0] + (fix[0, 0] - edge)
+            cur[0] = new
+            cur[1] = cur[1] + (fix[0, 1] - inner)
+            edge_out[r + 1] = new
+            send_edges(r + 1)
+
+        @pl.when(r == 3)
+        def _():
+            low = lax.broadcasted_iota(jnp.int32, (vals, LANES), 1) < HALF
+            for ref, e, i in ((base_ref, cur[0], cur[1]), (step_ref, fix[0, 0] - edge, fix[0, 1] - inner)):
+                turned = swap(i)
+                ref[:, :LANES] = jnp.where(low, e, turned)
+                ref[:, LANES:] = jnp.where(low, turned, e)
+
+        return carry
+
+    lax.fori_loop(0, 4, sweep, 0)
 
     over(groups, lambda off: to_group(off).wait_send())
     over(curves, lambda off: to_curve(off).wait_send())
@@ -408,24 +435,27 @@
         rdepth = restr.shape[0] * vals
         assert blocks == 2 * LANES and vals == HALF
         vm = pltpu.VMEM
-        return pl.pallas_call(
+        base, step = pl.pallas_call(
             functools.partial(kernel, curves, groups, len(args)),
-            out_shape=jax.ShapeDtypeStruct(rhs.shape, F32),
+            out_shape=[jax.ShapeDtypeStruct(rhs.shape, F32)] * 2,
             in_specs=[pl.BlockSpec(memory_space=pltpu.HBM)] * len(args),
-            out_specs=pl.BlockSpec(memory_space=pltpu.VMEM),
+            out_specs=[pl.BlockSpec(memory_space=pltpu.VMEM)] * 2,
             scratch_shapes=[vm(a.shape, a.dtype) for a in args] + [
                 pltpu.SemaphoreType.DMA((len(args),)),
-                vm((2 * vals, depth), BF16),
-                vm((2 * vals, depth), BF16),
+                vm((2, 2 * vals, depth), BF16),
                 vm((depth, 2 * LANES), BF16),
                 vm((2 * vals, rdepth), BF16),
                 vm((2 * vals, rdepth), BF16),
                 vm((2 * vals, vals), BF16),
-                vm((8, cw), jnp.int32),
-                vm((8, cw), jnp.int32),
-                vm((8, cw), jnp.int32),
+                vm((cw // LANES, 8, LANES), jnp.int32),
+                vm((cw // LANES, 8, LANES), jnp.int32),
+                vm((cw // LANES, 8, LANES), jnp.int32),
+                vm((2, cw // LANES, vals, LANES), F32),
                 vm((cw // LANES, vals, LANES), F32),
                 vm((cw, LANES), F32),
+                vm((2, vals, LANES), F32),
+                vm((2, vals, LANES), F32),
+                vm((3, 2, vals, LANES), F32),
                 vm((4, vals, LANES), F32),
                 vm((4, vals, LANES), F32),
                 vm((4, vals, LANES), F32),
@@ -443,6 +473,7 @@
                 collective_id=0, has_side_effects=True, vmem_limit_bytes=60 * 2**20
             ),
         )(*args)
+        return base + step
 
     fine, part, all_ = P(None, ("curve", "group")), P(None, "curve"), P()
     return jax.shard_map(

time: 35.8 us -> 35.7 us (level)
  other arithmetic: 0 us -> 1.51 us
  local copies, waits for them, and re-layouts: 1.47 us -> 0 us
    add x0 -> x1, other arithmetic: none -> 1.51 us  [shards(): return base + step]
    unnamed x1 -> x0, local copies, waits for them, and re-layouts: 1.47 us -> none
where the time goes in v2:
time: 35.7 us; the launch traced here: 35.5 us
  Pallas kernels  34 us (95%)
  other arithmetic  1.51 us (4%)
    pallas_call x1, Pallas kernels, shards(): pl.pallas_call(functools.partial(kernel, curves, groups, len(args)), out_...  34 us
    add x1, other arithmetic, shards(): return base + step  1.51 us

profile of v2, /device:TPU:1, one launch (start us, length us, event | category | flops | bytes accessed | tf_op | source)
XLA Modules:
  0.0 35.5 jit_solution(12812462989902648632)
XLA Ops:
  0.0 34.0 %shard_map.154 = (f32[64,256]{1,0:T(8,128)}, f32[64,256]{1,0:T(8,128)}) custom-call(f32[64,256]{1,0:T(8,128)} %refs_0_.1, f32[64,256]{1,0:T(8,128)} %refs_1_.1, s32[1,256]{1,0:T(1,128)} %bitcast.2, s32[8,256]{1,0:T(8,128)} %refs_3_.1, s32[8,256]{1,0:T(8,128)} %refs_4_.1, s32[2,256]{1,0:T(2,128)} %refs_5_.1, s32[2,256]{1,0:T(2,128)} %refs_6_.1, ...), custom_call_target="tpu_custom_call" | custom-call | tf_op jit(solution)/shard_map/pallas_call | solution.py:438
  34.0 1.5 %add.3 = f32[64,256]{1,0:T(8,128)} add(f32[64,256]{1,0:T(8,128)} %get-tuple-element.7, f32[64,256]{1,0:T(8,128)} %get-tuple-element.8) | non-fusion elementwise | flops 16384 | bytes 196608 | tf_op jit(solution)/shard_map/add | solution.py:476

commit v3 on v2

--- a/solution.py
+++ b/solution.py
@@ -104,7 +104,7 @@
     rhs_ref, start_ref, level_ref, nbr_ref, kind_ref, own0_ref, own1_ref, own2_ref, own3_ref,
     cnbr_ref, ckind_ref, clevel_ref, stiff_ref, smooth_ref, coup_ref, restr_ref,
     base_ref, step_ref,
-    mats, gst, rst, rtst, sst, cnb, ckd, clv, cfield, crhs, crow, cur, res, fix,
+    mats, rst, rtst, sst, cnb, ckd, clv, cfield, crhs, crow, cur, res, fix,
     edge_out, from_prev, from_next, part, gpart, hpart,
     esend, erecv, gsend, grecv, hsend, hrecv,
 ):
@@ -157,7 +157,6 @@
     loads[1].wait()
     start_e, start_i = edge_inner(start_ref)
     edge_out[0] = start_e
-    pl.semaphore_wait(barrier, groups + curves - 2 + has_prev.astype(jnp.int32) + has_next.astype(jnp.int32))
 
     def to_prev(r):
         return pltpu.make_async_remote_copy(
@@ -190,7 +189,6 @@
         low = lax.broadcasted_iota(jnp.int32, (vals, LANES), 1) < HALF
         return jnp.where(low, from_next[r], from_prev[r])
 
-    send_edges(0)
     for n, load in enumerate(loads):
         if n != 1:
             load.wait()
@@ -208,9 +206,8 @@
         cols = slice(i * LANES, (i + 1) * LANES)
         rst[:, cols] = stack(jnp.concatenate([one, two], axis=1))
         rtst[:, cols] = stack(jnp.concatenate([one.T, two.T], axis=1))
-    pad = gst.shape[0] - (kinds_n + 1) * vals
-    if pad:
-        gst[(kinds_n + 1) * vals:, :] = jnp.zeros((pad, 2 * LANES), BF16)
+    pl.semaphore_wait(barrier, groups + curves - 2 + has_prev.astype(jnp.int32) + has_next.astype(jnp.int32))
+    send_edges(0)
 
     rhs_e, rhs_i = edge_inner(rhs_ref)
     lev_e, lev_i = edge_inner(level_ref)
@@ -235,34 +232,50 @@
                 whole = whole + jnp.where(same, picked[other], 0.0)
             parts.append(stack(whole))
             codes.append(jnp.broadcast_to(kinds[k:k + 1].astype(F32), (2 * vals, LANES)).astype(BF16))
-        for t in range(kinds_n):
-            acc = jnp.zeros_like(parts[0])
+        empty = jnp.zeros_like(parts[0])
+
+        def of_kind(t):
+            if t >= kinds_n:
+                return stack(own) if t == kinds_n else empty
+            acc = empty
             for k in range(slots_n):
                 acc = jnp.where(codes[k] == jnp.asarray(t, BF16), parts[k], acc)
-            gst[t * vals:(t + 1) * vals, :LANES] = acc[:vals]
-            gst[t * vals:(t + 1) * vals, LANES:] = acc[vals:]
-        gst[kinds_n * vals:(kinds_n + 1) * vals, :] = side(own)
-        return fold(jnp.dot(left[...], gst[...], preferred_element_type=F32))
+            return acc
+
+        totals = [None, None]
+        chunk = 4
+        for c in range(left.shape[1] // (chunk * vals)):
+            found = [of_kind(t) for t in range(c * chunk, (c + 1) * chunk)]
+            right = jnp.concatenate([
+                jnp.concatenate([f[:vals] for f in found], axis=0),
+                jnp.concatenate([f[vals:] for f in found], axis=0)], axis=1)
+            r = jnp.dot(left[:, c * chunk * vals:(c + 1) * chunk * vals], right, preferred_element_type=F32)
+            totals[c % 2] = r if totals[c % 2] is None else totals[c % 2] + r
+        return fold(totals[0] + totals[1])
 
     def wide(row):
         return jnp.broadcast_to(row, (vals, LANES))
 
+    def places(at):
+        inner = (at >= HALF) & (at < HALF + LANES)
+        own = (at >= 0) & (at < 2 * LANES)
+        lane = at & (LANES - 1)
+        return jnp.where(inner, lane ^ HALF, lane), jnp.where(inner, 1, jnp.where(own, 0, 2))
+
+    lane_i, tile_i = places(at_i)
+    lane_e, tile_e = places(at_e)
+
     def inner_image(left, e, i):
         def picks(k):
-            at = wide(at_i[k:k + 1])
-            lane = at & (LANES - 1)
-            is_inner = (at >= HALF) & (at < HALF + LANES)
-            return jnp.where(is_inner, lane_take(i, lane ^ HALF), lane_take(e, lane))
+            lane = wide(lane_i[k:k + 1])
+            return jnp.where(wide(tile_i[k:k + 1]) == 1, lane_take(i, lane), lane_take(e, lane))
         return couple(left, i, kind_i, picks)
 
     def edge_image(left, e, i, h):
         def picks(k):
-            at = wide(at_e[k:k + 1])
-            lane = at & (LANES - 1)
-            is_inner = (at >= HALF) & (at < HALF + LANES)
-            is_own = (at >= 0) & (at < 2 * LANES)
-            got = jnp.where(is_own, lane_take(e, lane), lane_take(h, lane))
-            return jnp.where(is_inner, lane_take(i, lane ^ HALF), got)
+            lane, tile = wide(lane_e[k:k + 1]), wide(tile_e[k:k + 1])
+            got = jnp.where(tile == 0, lane_take(e, lane), lane_take(h, lane))
+            return jnp.where(tile == 1, lane_take(i, lane), got)
         return couple(left, e, kind_e, picks)
 
     fix[0, 0], fix[0, 1] = times(sst[...], gs_e), times(sst[...], gs_i)
@@ -430,7 +443,7 @@
         rhs, coup, restr = args[0], args[14], args[15]
         vals, blocks = rhs.shape
         kinds = coup.shape[0] + 1
-        depth = (kinds + kinds % 2) * vals
+        depth = -(-kinds // 4) * 4 * vals
         cw = -(-args[9].shape[1] // LANES) * LANES
         rdepth = restr.shape[0] * vals
         assert blocks == 2 * LANES and vals == HALF
@@ -443,7 +456,6 @@
             scratch_shapes=[vm(a.shape, a.dtype) for a in args] + [
                 pltpu.SemaphoreType.DMA((len(args),)),
                 vm((2, 2 * vals, depth), BF16),
-                vm((depth, 2 * LANES), BF16),
                 vm((2 * vals, rdepth), BF16),
                 vm((2 * vals, rdepth), BF16),
                 vm((2 * vals, vals), BF16),

time: 35.7 us -> 34.9 us (0.978)
  Pallas kernels: 34 us -> 33.2 us
    pallas_call x1, Pallas kernels: 34 us -> 33.2 us  [shards(): pl.pallas_call(functools.partial(kernel, curves, groups, len(args)), out_...]
where the time goes in v3:
time: 34.9 us; the launch traced here: 34.7 us
  Pallas kernels  33.2 us (95%)
  other arithmetic  1.51 us (4%)
    pallas_call x1, Pallas kernels, shards(): pl.pallas_call(functools.partial(kernel, curves, groups, len(args)), out_...  33.2 us
    add x1, other arithmetic, shards(): return base + step  1.51 us

profile of v3, /device:TPU:1, one launch (start us, length us, event | category | flops | bytes accessed | tf_op | source)
XLA Modules:
  0.0 34.7 jit_solution(16454193743712895331)
XLA Ops:
  0.0 33.2 %shard_map.154 = (f32[64,256]{1,0:T(8,128)}, f32[64,256]{1,0:T(8,128)}) custom-call(f32[64,256]{1,0:T(8,128)} %refs_0_.1, f32[64,256]{1,0:T(8,128)} %refs_1_.1, s32[1,256]{1,0:T(1,128)} %bitcast.2, s32[8,256]{1,0:T(8,128)} %refs_3_.1, s32[8,256]{1,0:T(8,128)} %refs_4_.1, s32[2,256]{1,0:T(2,128)} %refs_5_.1, s32[2,256]{1,0:T(2,128)} %refs_6_.1, ...), custom_call_target="tpu_custom_call" | custom-call | tf_op jit(solution)/shard_map/pallas_call | solution.py:451
  33.2 1.5 %add.3 = f32[64,256]{1,0:T(8,128)} add(f32[64,256]{1,0:T(8,128)} %get-tuple-element.7, f32[64,256]{1,0:T(8,128)} %get-tuple-element.8) | non-fusion elementwise | flops 16384 | bytes 196608 | tf_op jit(solution)/shard_map/add | solution.py:488

commit v4 on v3

--- a/solution.py
+++ b/solution.py
@@ -293,7 +293,10 @@
     at_three = jnp.where(lane_at < per_three, me_c * per_three + lane_at, 0)
     par3, oct3 = row_take(own3_ref, 0, at_three), row_take(own3_ref, 1, at_three)
 
-    width = cnbr_ref.shape[1]
+    slots_all, width = cnbr_ref.shape
+    rep = LANES // width if width < LANES and LANES % width == 0 else 1
+    rep = rep if slots_all % rep == 0 else 1
+    rows_n = slots_all // rep
     cnb[...] = jnp.full_like(cnb, -1)
     ckd[...] = jnp.full_like(ckd, -1)
     clv[...] = jnp.zeros_like(clv)
@@ -301,8 +304,10 @@
     for n in range(ctiles):
         size = min(LANES, width - n * LANES)
         cols = slice(n * LANES, n * LANES + size)
-        cnb[n, :, :size] = cnbr_ref[:, cols]
-        ckd[n, :, :size] = ckind_ref[:, cols]
+        for g in range(rep):
+            rows, place = slice(g * rows_n, (g + 1) * rows_n), slice(g * size, (g + 1) * size)
+            cnb[n, :rows_n, place] = cnbr_ref[rows, cols]
+            ckd[n, :rows_n, place] = ckind_ref[rows, cols]
         clv[n, :, :size] = jnp.broadcast_to(clevel_ref[:, cols], (8, size))
 
     def to_group(off):
@@ -331,9 +336,10 @@
         slots = jnp.where(ids == par3[0:1], 1.0, 0.0).astype(BF16)
         hi, lo = split(mapped)
         zeros = jnp.zeros_like(hi)
-        part[...] = (lax.dot_general(slots, jnp.concatenate([hi, zeros], axis=0), NT, preferred_element_type=F32)
+        sums = (lax.dot_general(slots, jnp.concatenate([hi, zeros], axis=0), NT, preferred_element_type=F32)
                      + lax.dot_general(slots, jnp.concatenate([lo, zeros], axis=0), NT, preferred_element_type=F32))
 
+        part[...] = sums[:per_four]
         over(groups, lambda off: to_group(off).start())
         over(groups, lambda off: to_group(off).wait_recv())
         mine = part[...]
@@ -344,7 +350,7 @@
         over(curves, lambda off: from_curve(off).wait_recv())
 
         for m in range(curves):
-            crow[m * per_four:(m + 1) * per_four, :] = hpart[m, :per_four, :]
+            crow[m * per_four:(m + 1) * per_four, :] = hpart[m]
         for n in range(ctiles):
             block = crow[n * LANES:(n + 1) * LANES, :].T[:vals]
             crhs[n] = times(sst[...], block * jnp.exp2(clv[n, 0:1].astype(F32)))
@@ -353,8 +359,8 @@
         def coarse_step(s, carry):
             sweep, n = s // ctiles, lax.rem(s, ctiles)
             old = lax.rem(sweep, 2)
-            at_c = cnb[n]
-            kind_c = jnp.where(at_c >= 0, ckd[n], -1)
+            at_c = cnb[n, :rows_n]
+            kind_c = jnp.where(at_c >= 0, ckd[n, :rows_n], -1)
             field = [cfield[old, m] for m in range(ctiles)]
             own = cfield[old, n]
 
@@ -366,7 +372,14 @@
                     got = jnp.where((at >> 7) == m, lane_take(field[m], lane), got)
                 return got
 
-            cfield[1 - old, n] = own + (crhs[n] - couple(mats.at[0], own, kind_c, picks))
+            once = own
+            if rep > 1:
+                once = jnp.where(lax.broadcasted_iota(jnp.int32, own.shape, 1) < width, own, 0.0)
+            image = couple(mats.at[0], once, kind_c, picks)
+            total = image
+            for g in range(1, rep):
+                total = total + pltpu.roll(image, g * width, 1)
+            cfield[1 - old, n] = own + (crhs[n] - total)
             return carry
 
         lax.fori_loop(0, (COARSE_SWEEPS - 1) * ctiles, coarse_step, 0)
@@ -445,6 +458,7 @@
         kinds = coup.shape[0] + 1
         depth = -(-kinds // 4) * 4 * vals
         cw = -(-args[9].shape[1] // LANES) * LANES
+        four = args[9].shape[1] // curves
         rdepth = restr.shape[0] * vals
         assert blocks == 2 * LANES and vals == HALF
         vm = pltpu.VMEM
@@ -471,9 +485,9 @@
                 vm((4, vals, LANES), F32),
                 vm((4, vals, LANES), F32),
                 vm((4, vals, LANES), F32),
-                vm((8, LANES), F32),
-                vm((groups, 8, LANES), F32),
-                vm((curves, 8, LANES), F32),
+                vm((four, LANES), F32),
+                vm((groups, four, LANES), F32),
+                vm((curves, four, LANES), F32),
                 pltpu.SemaphoreType.DMA((4, 2)),
                 pltpu.SemaphoreType.DMA((4, 2)),
                 pltpu.SemaphoreType.DMA((groups,)),

time: 34.9 us -> 34.4 us (0.986)
  Pallas kernels: 33.2 us -> 32.7 us
    pallas_call x1, Pallas kernels: 33.2 us -> 32.7 us  [shards(): pl.pallas_call(functools.partial(kernel, curves, groups, len(args)), out_...]
where the time goes in v4:
time: 34.4 us; the launch traced here: 34.2 us
  Pallas kernels  32.7 us (95%)
  other arithmetic  1.51 us (4%)
    pallas_call x1, Pallas kernels, shards(): pl.pallas_call(functools.partial(kernel, curves, groups, len(args)), out_...  32.7 us
    add x1, other arithmetic, shards(): return base + step  1.51 us

profile of v4, /device:TPU:1, one launch (start us, length us, event | category | flops | bytes accessed | tf_op | source)
XLA Modules:
  0.0 34.2 jit_solution(14679886759600809747)
XLA Ops:
  0.0 32.7 %shard_map.154 = (f32[64,256]{1,0:T(8,128)}, f32[64,256]{1,0:T(8,128)}) custom-call(f32[64,256]{1,0:T(8,128)} %refs_0_.1, f32[64,256]{1,0:T(8,128)} %refs_1_.1, s32[1,256]{1,0:T(1,128)} %bitcast.2, s32[8,256]{1,0:T(8,128)} %refs_3_.1, s32[8,256]{1,0:T(8,128)} %refs_4_.1, s32[2,256]{1,0:T(2,128)} %refs_5_.1, s32[2,256]{1,0:T(2,128)} %refs_6_.1, ...), custom_call_target="tpu_custom_call" | custom-call | tf_op jit(solution)/shard_map/pallas_call | solution.py:465
  32.7 1.5 %add.3 = f32[64,256]{1,0:T(8,128)} add(f32[64,256]{1,0:T(8,128)} %get-tuple-element.7, f32[64,256]{1,0:T(8,128)} %get-tuple-element.8) | non-fusion elementwise | flops 16384 | bytes 196608 | tf_op jit(solution)/shard_map/add | solution.py:502

commit v5 on v4

--- a/solution.py
+++ b/solution.py
@@ -121,6 +121,14 @@
     per_four = cnbr_ref.shape[1] // curves
     ctiles = cfield.shape[1]
 
+    half = vals // 2
+    low_half = lax.broadcasted_iota(jnp.int32, (half, LANES), 1) < HALF
+
+    def pack_edges(r, e):
+        turned = swap(e[half:])
+        edge_out[r, 0] = jnp.where(low_half, e[:half], turned)
+        edge_out[r, 1] = jnp.where(low_half, turned, e[:half])
+
     @pl.when(jnp.logical_not(has_prev))
     def _():
         from_prev[...] = jnp.zeros_like(from_prev)
@@ -156,16 +164,16 @@
     over(curves, lambda off: greet((lax.rem(me_c + off, curves), me_g)))
     loads[1].wait()
     start_e, start_i = edge_inner(start_ref)
-    edge_out[0] = start_e
+    pack_edges(0, start_e)
 
     def to_prev(r):
         return pltpu.make_async_remote_copy(
-            src_ref=edge_out.at[r], dst_ref=from_next.at[r], send_sem=esend.at[r, 0],
+            src_ref=edge_out.at[r, 0], dst_ref=from_next.at[r], send_sem=esend.at[r, 0],
             recv_sem=erecv.at[r, 0], device_id=prev_id, device_id_type=MESH)
 
     def to_next(r):
         return pltpu.make_async_remote_copy(
-            src_ref=edge_out.at[r], dst_ref=from_prev.at[r], send_sem=esend.at[r, 1],
+            src_ref=edge_out.at[r, 1], dst_ref=from_prev.at[r], send_sem=esend.at[r, 1],
             recv_sem=erecv.at[r, 1], device_id=next_id, device_id_type=MESH)
 
     def send_edges(r):
@@ -186,8 +194,9 @@
         def _():
             to_next(r).wait_recv()
 
-        low = lax.broadcasted_iota(jnp.int32, (vals, LANES), 1) < HALF
-        return jnp.where(low, from_next[r], from_prev[r])
+        after, before = from_next[r], from_prev[r]
+        return jnp.concatenate(
+            [jnp.where(low_half, after, before), swap(jnp.where(low_half, before, after))], axis=0)
 
     for n, load in enumerate(loads):
         if n != 1:
@@ -393,7 +402,7 @@
         back = octant_dot(rtst[...], lane_take(back, wide(par2[0:1])), oct2[0:1])
         back = octant_dot(rtst[...], lane_take(back, wide(par1[0:1])), oct1[0:1])
         e = cur[0] + octant_dot(rtst[...], lane_take(back, wide(own0_e[0:1])), own0_e[1:2])
-        edge_out[3] = e
+        pack_edges(3, e)
         cur[0] = e
         send_edges(3)
         cur[1] = cur[1] + octant_dot(rtst[...], lane_take(back, wide(own0_i[0:1])), own0_i[1:2])
@@ -417,7 +426,7 @@
             new = cur[0] + (fix[0, 0] - edge)
             cur[0] = new
             cur[1] = cur[1] + (fix[0, 1] - inner)
-            edge_out[r + 1] = new
+            pack_edges(r + 1, new)
             send_edges(r + 1)
 
         @pl.when(r == 3)
@@ -482,9 +491,9 @@
                 vm((2, vals, LANES), F32),
                 vm((2, vals, LANES), F32),
                 vm((3, 2, vals, LANES), F32),
-                vm((4, vals, LANES), F32),
-                vm((4, vals, LANES), F32),
-                vm((4, vals, LANES), F32),
+                vm((4, 2, vals // 2, LANES), F32),
+                vm((4, vals // 2, LANES), F32),
+                vm((4, vals // 2, LANES), F32),
                 vm((four, LANES), F32),
                 vm((groups, four, LANES), F32),
                 vm((curves, four, LANES), F32),

time: 34.4 us -> 34 us (0.988)
  Pallas kernels: 32.7 us -> 32.3 us
    pallas_call x1, Pallas kernels: 32.7 us -> 32.3 us  [shards(): pl.pallas_call(functools.partial(kernel, curves, groups, len(args)), out_...]
where the time goes in v5:
time: 34 us; the launch traced here: 33.8 us
  Pallas kernels  32.3 us (95%)
  other arithmetic  1.51 us (4%)
    pallas_call x1, Pallas kernels, shards(): pl.pallas_call(functools.partial(kernel, curves, groups, len(args)), out_...  32.3 us
    add x1, other arithmetic, shards(): return base + step  1.51 us

profile of v5, /device:TPU:1, one launch (start us, length us, event | category | flops | bytes accessed | tf_op | source)
XLA Modules:
  0.0 33.8 jit_solution(17593576661038299658)
XLA Ops:
  0.0 32.3 %shard_map.154 = (f32[64,256]{1,0:T(8,128)}, f32[64,256]{1,0:T(8,128)}) custom-call(f32[64,256]{1,0:T(8,128)} %refs_0_.1, f32[64,256]{1,0:T(8,128)} %refs_1_.1, s32[1,256]{1,0:T(1,128)} %bitcast.2, s32[8,256]{1,0:T(8,128)} %refs_3_.1, s32[8,256]{1,0:T(8,128)} %refs_4_.1, s32[2,256]{1,0:T(2,128)} %refs_5_.1, s32[2,256]{1,0:T(2,128)} %refs_6_.1, ...), custom_call_target="tpu_custom_call" | custom-call | tf_op jit(solution)/shard_map/pallas_call | solution.py:474
  32.3 1.5 %add.3 = f32[64,256]{1,0:T(8,128)} add(f32[64,256]{1,0:T(8,128)} %get-tuple-element.7, f32[64,256]{1,0:T(8,128)} %get-tuple-element.8) | non-fusion elementwise | flops 16384 | bytes 196608 | tf_op jit(solution)/shard_map/add | solution.py:511
